TPU v7x, 256 devices: a whole 4x4x8 slice. The times are simulated.
256 devices in a mesh: blk: 64 (over x, y, z_hi), rep: 4 (over z_lo, core).
Axes of the slice: x: 4, y: 4, z: 8 (z_hi: 4, z_lo: 2; z = z_hi * 2 + z_lo), core: 2. Of those that a mesh axis runs over, the one named last changes fastest.
Arguments:
- row_embed: float32 [131072, 300], P(('blk', 'rep')), may hold values from -1.5 to 1.5
- col_embed: float32 [131072, 300], P(('blk', 'rep')), may hold values from -1.5 to 1.5
- counts: int32 [2, 131072, 2048], P(None, ('blk', 'rep')), may hold values from 0 to 199, as said below
- log_marginal: float32 [131072], replicated, may hold values from 8 to 12
Outputs:
- rows_after: float32 [131072, 300], P(('blk', 'rep'))
- cols_after: float32 [131072, 300], P(('blk', 'rep'))
Inputs may be any that keep to these rules, and one draw needn't show every extreme that they name: About half the counts are zero; the rest are spread evenly.
All inputs are finite; a program needn't handle non-finite values.
Results may differ from a plain program's by a relative error of at most 0.0029.
Values may be sent and summed in bfloat16 or wider, within the bound.
A program may use at most 64 MiB of HBM per device.

v0:
```python
import jax
import jax.numpy as jnp
from jax import lax
from jax.sharding import PartitionSpec as P

step_size = 0.05


def swapped(value, axis, apart):
    mask = 2**apart
    pairs = [(source, source ^ mask) for source in range(lax.axis_size(axis))]
    return lax.ppermute(value, axis, pairs)


def slope_of(pred, count_int, pmi, scale):
    count = count_int.astype(jnp.float32)
    confidence = 0.1 + 0.25 * jnp.sqrt(count)
    target = jnp.log(jnp.maximum(count, 1.0)) + pmi
    slope = jnp.where(count_int > 0, confidence * (pred - target), jax.nn.sigmoid(pred - pmi))
    return (slope * scale).astype(jnp.bfloat16)


def fit_round(rows, cols, tile_counts, log_marginal, log_total, swap_bit):
    rep_count = lax.axis_size("rep")
    own_block = lax.axis_index("blk")
    own_part = lax.axis_index("rep")
    local_rows = rows.shape[0]
    block_rows = local_rows * rep_count
    partner = jnp.bitwise_xor(own_block, 1 << swap_bit)
    row_half = rows.astype(jnp.bfloat16)
    col_half = cols.astype(jnp.bfloat16)
    whole_block = lax.all_gather(col_half, "rep", axis=0, tiled=True)
    partner_cols = swapped(whole_block, "blk", swap_bit)
    row_margin = lax.dynamic_slice_in_dim(
        log_marginal, (own_block * rep_count + own_part) * local_rows, local_rows
    )
    col_margin = lax.dynamic_slice_in_dim(log_marginal, partner * block_rows, block_rows)
    pred = lax.dot_general(
        row_half, partner_cols, (((1,), (1,)), ((), ())), preferred_element_type=jnp.float32
    )
    pmi = log_total - row_margin[:, None] - col_margin[None, :]
    scale = 1.0 / jnp.sqrt(jnp.float32(block_rows))
    slope = slope_of(pred, tile_counts, pmi, scale)
    row_grad = jnp.dot(slope, partner_cols, preferred_element_type=jnp.float32)
    far_grad = lax.dot_general(
        slope, row_half, (((0,), (0,)), ((), ())), preferred_element_type=jnp.float32
    )
    summed = lax.psum_scatter(far_grad, "rep", scatter_dimension=0, tiled=True)
    col_grad = swapped(summed, "blk", swap_bit)
    return (row_grad, col_grad)


def per_device(row_embed, col_embed, counts, log_marginal):
    log_total = jax.nn.logsumexp(log_marginal)
    rows, cols = (row_embed, col_embed)
    bits = [lax.axis_size("blk").bit_length() - 2, 0]
    for rnd in range(counts.shape[0]):
        row_grad, col_grad = fit_round(rows, cols, counts[rnd], log_marginal, log_total, bits[rnd])
        rows = rows - step_size * row_grad
        cols = cols - step_size * col_grad
    return (rows, cols)


def solution(mesh):
    placed = (P(("blk", "rep"), None), P(("blk", "rep"), None), P(None, ("blk", "rep"), None), P())
    return jax.shard_map(
        per_device,
        mesh=mesh,
        in_specs=placed,
        out_specs=(P(("blk", "rep"), None), P(("blk", "rep"), None)),
        check_vma=False,
    )
```

profile of v0, /device:TPU:16, one launch (start us, length us, event | category | flops | bytes accessed | tf_op | source)
XLA Modules:
  0.0 296.8 jit_solution(14370645651436058044)
XLA Ops:
  7.2 1.8 convert_element_type.28
  9.1 28.8 %all-gather.3.cloned.1.call-done = bf16[2048,300]{0,1:T(8,128)(2,1)} async-done(((bf16[512,300]{0,1:T(8,128)(2,1)}), bf16[2048,300]{0,1:T(8,128)(2,1)}) %all-gather.3.cloned.1.call-update) | async-done | bytes 1228816 | tf_op jit(solution)/shard_map/all_gather | solution.py:32
  37.9 3.0 %collective-permute-start = (bf16[2048,300]{0,1:T(8,128)(2,1)}, bf16[2048,300]{0,1:T(8,128)(2,1)S(1)}, u32[]{:S(2)}, u32[]{:S(2)}) collective-permute-start(bf16[2048,300]{0,1:T(8,128)(2,1)} %all-gather.3.cloned.1.call-done), channel_id=1, source_target_pairs={{0,128},{4,132},{8,136},{12,140},{16,144},{20,148},{24,152},{28,15... | collective-permute-start | bytes 3686408 | tf_op jit(solution)/shard_map/ppermute | solution.py:12
  40.9 1.8 reduce_max.9
  44.0 1.8 exponential_reduce_fusion
  48.0 21.2 %collective-permute-done = bf16[2048,300]{0,1:T(8,128)(2,1)S(1)} collective-permute-done((bf16[2048,300]{0,1:T(8,128)(2,1)}, bf16[2048,300]{0,1:T(8,128)(2,1)S(1)}, u32[]{:S(2)}, u32[]{:S(2)}) %collective-permute-start) | collective-permute-done | bytes 1228832 | tf_op jit(solution)/shard_map/ppermute | solution.py:12
  69.2 1.1 copy-done.3
  70.3 7.0 %fusion.4 = bf16[512,2048]{1,0:T(8,128)(2,1)S(1)} fusion(s32[2,512,2048]{2,1,0:T(8,128)} %param.6, f32[2048]{0:T(1024)S(1)} %get-tuple-element.3, f32[512]{0:T(512)S(1)} %dynamic-slice_subtract_fusion, bf16[2048,300]{0,1:T(8,128)(2,1)} %copy-done.3, f32[512,300]{0,1:T(8,128)} %param.4), kind=kOutput, calls=%fused_computation.8 | convolution fusion | flops 646076416 | bytes 8144896 | tf_op jit(solution)/shard_map/dot_general | solution.py:38
  77.3 2.3 fusion.24
  79.7 34.6 %reduce-scatter.3.cloned.1.call-done = f32[512,300]{0,1:T(8,128)} async-done(((f32[2048,300]{0,1:T(8,128)}), f32[512,300]{0,1:T(8,128)}) %reduce-scatter.3.cloned.1.call-update) | async-done | bytes 614416 | tf_op jit(solution)/shard_map/reduce_scatter | solution.py:48
  114.3 3.0 collective-permute-start.1
  117.2 14.8 %collective-permute-done.1 = f32[512,300]{0,1:T(8,128)S(1)} collective-permute-done((f32[512,300]{0,1:T(8,128)}, f32[512,300]{0,1:T(8,128)S(1)}, u32[]{:S(2)}, u32[]{:S(2)}) %collective-permute-start.1) | collective-permute-done | bytes 614432 | tf_op jit(solution)/shard_map/ppermute | solution.py:12
  132.0 0.9 fusion.20
  133.0 25.2 %all-gather.5.cloned.1.call-done = bf16[2048,300]{0,1:T(8,128)(2,1)} async-done(((bf16[512,300]{0,1:T(8,128)(2,1)}), bf16[2048,300]{0,1:T(8,128)(2,1)}) %all-gather.5.cloned.1.call-update) | async-done | bytes 1228816 | tf_op jit(solution)/shard_map/all_gather | solution.py:32
  158.2 2.5 collective-permute-start.2
  160.7 2.3 fusion.18
  163.1 52.4 %collective-permute-done.2 = bf16[2048,300]{0,1:T(8,128)(2,1)S(1)} collective-permute-done((bf16[2048,300]{0,1:T(8,128)(2,1)}, bf16[2048,300]{0,1:T(8,128)(2,1)S(1)}, u32[]{:S(2)}, u32[]{:S(2)}) %collective-permute-start.2) | collective-permute-done | bytes 1228832 | tf_op jit(solution)/shard_map/ppermute | solution.py:12
  215.4 6.4 %fusion.13 = bf16[512,2048]{1,0:T(8,128)(2,1)S(1)} fusion(s32[2,512,2048]{2,1,0:T(8,128)} %param.6, f32[2048]{0:T(1024)S(1)} %get-tuple-element.2, f32[512]{0:T(512)S(1)} %dynamic-slice_subtract_fusion, bf16[2048,300]{0,1:T(8,128)(2,1)S(1)} %collective-permute-done.2, f32[512,300]{0,1:T(8,128)S(1)} %fusion.18), kind=kOutput, calls=%fused_computation.17 | convolution fusion | flops 646076416 | bytes 8144896 | tf_op jit(solution)/shard_map/dot_general | solution.py:38
  221.8 2.3 fusion.21
  224.2 34.7 %reduce-scatter.5.cloned.1.call-done = f32[512,300]{0,1:T(8,128)} async-done(((f32[2048,300]{0,1:T(8,128)}), f32[512,300]{0,1:T(8,128)}) %reduce-scatter.5.cloned.1.call-update) | async-done | bytes 614416 | tf_op jit(solution)/shard_map/reduce_scatter | solution.py:48
  258.8 2.6 collective-permute-start.3
  261.4 3.2 %fusion.19 = f32[512,300]{0,1:T(8,128)} fusion(f32[512,300]{0,1:T(8,128)} %copy-done.2, bf16[512,2048]{1,0:T(8,128)(2,1)S(1)} %fusion.13, bf16[2048,300]{0,1:T(8,128)(2,1)} %copy-done.4), kind=kOutput, calls=%fused_computation.25 | convolution fusion | flops 629452800 | bytes 4554752 | tf_op jit(solution)/shard_map/dot_general | solution.py:44
  264.6 24.7 %collective-permute-done.3 = f32[512,300]{0,1:T(8,128)S(1)} collective-permute-done((f32[512,300]{0,1:T(8,128)}, f32[512,300]{0,1:T(8,128)S(1)}, u32[]{:S(2)}, u32[]{:S(2)}) %collective-permute-start.3) | collective-permute-done | bytes 614432 | tf_op jit(solution)/shard_map/ppermute | solution.py:12
  289.2 1.0 multiply_subtract_fusion
  (19 shorter events, 1.7 us)
Async XLA Ops:
  7.2 30.8 %all-gather.3.cloned.1.call-start = ((), (), s32[]{:S(2)}) async-start(), calls=%async_computation.2 | async-start | bytes 1556480 | tf_op jit(solution)/shard_map/all_gather | solution.py:32
  9.1 105.2 %reduce-scatter.3.cloned.1.call-start = ((), (), s32[]{:S(2)}) async-start(), calls=%async_computation.3 | async-start | bytes 3112960 | tf_op jit(solution)/shard_map/reduce_scatter | solution.py:48
  37.9 31.3 %collective-permute-start = (bf16[2048,300]{0,1:T(8,128)(2,1)}, bf16[2048,300]{0,1:T(8,128)(2,1)S(1)}, u32[]{:S(2)}, u32[]{:S(2)}) collective-permute-start(bf16[2048,300]{0,1:T(8,128)(2,1)} %all-gather.3.cloned.1.call-done), channel_id=1, source_target_pairs={{0,128},{4,132},{8,136},{12,140},{16,144},{20,148},{24,152},{28,15... | collective-permute-start | bytes 3686408 | tf_op jit(solution)/shard_map/ppermute | solution.py:12
  69.2 1.1 copy-start.3
  70.3 7.1 %copy-start.1 = (f32[512,300]{0,1:T(8,128)S(1)}, f32[512,300]{0,1:T(8,128)}, u32[]{:S(2)}) copy-start(f32[512,300]{0,1:T(8,128)} %param.4) | copy-start | bytes 1843204
  77.3 54.7 %copy-start = (f32[512,300]{0,1:T(8,128)S(1)}, f32[512,300]{0,1:T(8,128)}, u32[]{:S(2)}) copy-start(f32[512,300]{0,1:T(8,128)} %param.5) | copy-start | bytes 1843204
  79.7 78.5 %all-gather.5.cloned.1.call-start = ((), (), s32[]{:S(2)}) async-start(), calls=%async_computation.4 | async-start | bytes 1556480 | tf_op jit(solution)/shard_map/all_gather | solution.py:32
  114.3 17.8 %collective-permute-start.1 = (f32[512,300]{0,1:T(8,128)}, f32[512,300]{0,1:T(8,128)S(1)}, u32[]{:S(2)}, u32[]{:S(2)}) collective-permute-start(f32[512,300]{0,1:T(8,128)} %reduce-scatter.3.cloned.1.call-done), channel_id=1, source_target_pairs={{0,128},{4,132},{8,136},{12,140},{16,144},{20,148},{24,152},{28,15... | collective-permute-start | bytes 1843208 | tf_op jit(solution)/shard_map/ppermute | solution.py:12
  132.9 125.9 %reduce-scatter.5.cloned.1.call-start = ((), (), s32[]{:S(2)}) async-start(), calls=%async_computation.5 | async-start | bytes 3112960 | tf_op jit(solution)/shard_map/reduce_scatter | solution.py:48
  158.2 57.3 %collective-permute-start.2 = (bf16[2048,300]{0,1:T(8,128)(2,1)}, bf16[2048,300]{0,1:T(8,128)(2,1)S(1)}, u32[]{:S(2)}, u32[]{:S(2)}) collective-permute-start(bf16[2048,300]{0,1:T(8,128)(2,1)} %all-gather.5.cloned.1.call-done), channel_id=1, source_target_pairs={{0,4},{4,0},{8,12},{12,8},{16,20},{20,16},{24,28},{28,24},{32,36},... | collective-permute-start | bytes 3686408 | tf_op jit(solution)/shard_map/ppermute | solution.py:12
  163.1 58.8 %copy-start.2 = (f32[512,300]{0,1:T(8,128)}, f32[512,300]{0,1:T(8,128)S(1)}, u32[]{:S(2)}) copy-start(f32[512,300]{0,1:T(8,128)S(1)} %fusion.18) | copy-start | bytes 1843204
  215.4 6.4 %copy-start.4 = (bf16[2048,300]{0,1:T(8,128)(2,1)}, bf16[2048,300]{0,1:T(8,128)(2,1)S(1)}, u32[]{:S(2)}) copy-start(bf16[2048,300]{0,1:T(8,128)(2,1)S(1)} %collective-permute-done.2) | copy-start | bytes 3686404
  258.8 30.4 %collective-permute-start.3 = (f32[512,300]{0,1:T(8,128)}, f32[512,300]{0,1:T(8,128)S(1)}, u32[]{:S(2)}, u32[]{:S(2)}) collective-permute-start(f32[512,300]{0,1:T(8,128)} %reduce-scatter.5.cloned.1.call-done), channel_id=1, source_target_pairs={{0,4},{4,0},{8,12},{12,8},{16,20},{20,16},{24,28},{28,24},{32,36},... | collective-permute-start | bytes 1843208 | tf_op jit(solution)/shard_map/ppermute | solution.py:12
Sparse Core Ops, SparseCore 0:
  10.4 27.4 all-gather.2
  79.8 34.4 reduce-scatter.2
  133.0 25.0 all-gather.4
  224.3 34.4 reduce-scatter.4
where the time goes:
time: 298 us; the launch traced here: 297 us
  waiting for transfers between devices  236 us (79%)
  matrix products  23.6 us (8%)
  between operations  15.8 us (5%)
  starting transfers between devices  11.2 us (4%)
  other arithmetic  8.08 us (3%)
    ppermute x4, waiting for transfers between devices, swapped(): return lax.ppermute(value, axis, pairs)  113 us
    reduce_scatter x2, waiting for transfers between devices, fit_round(): summed = lax.psum_scatter(far_grad, 'rep', scatter_dimension=0, tiled=True)  69.2 us
    all_gather x2, waiting for transfers between devices, fit_round(): whole_block = lax.all_gather(col_half, 'rep', axis=0, tiled=True)  54 us
    dot_general x2, matrix products, fit_round(): lax.dot_general(row_half, partner_cols, (((1,), (1,)), ((), ())), preferr...  13.4 us
    ppermute x4, starting transfers between devices, swapped(): return lax.ppermute(value, axis, pairs)  11.1 us
  transfers between devices with their start and end apart: 8, of which 8 were waited for; matrix products, arithmetic and copies ran while one was open for 4% of the time, Pallas kernels for 0%

commit v1 on v0

v1 whole, which is shorter than its diff:
```python
import functools

import jax
import jax.numpy as jnp
from jax import lax
from jax.experimental import pallas as pl
from jax.experimental.pallas import tpu as pltpu
from jax.sharding import PartitionSpec as P

STEP = 0.05
PARTS = 4
CUTS = 4
MESH = pl.DeviceIdType.MESH
TO_PARTNER, TO_CORE, TO_NEAR, TO_CORE_FAR, PART_A, PART_B, SUM_NEAR, SUM_NEAR_FAR, TOTAL, TOTAL_FAR, TO_NEAR_FAR = range(11)
KINDS = 11


def other(bit):
    return 1 - bit


def kernel(
    n_blk, rounds, cuts, piece,
    rows_ref, cols_ref, counts_ref, margin_ref, rows_out, cols_out,
    counts, gain, shift, rows_f, rows_t, rows_n, row_grad, cols_f, row_margin,
    sent, came, part_own, part_out, part_in, near_out, near_in, total_out, total_in,
    count_sem, send_sem, came_sem, part_sem, near_sem, total_sem,
):
    width, local = rows_ref.shape
    padded = rows_f.shape[0]
    pieces = rounds * cuts
    blk = lax.axis_index("blk")
    rep = lax.axis_index("rep")
    near = rep // 2
    core = rep % 2
    high = n_blk // 2
    inner = (blk + near) % 2 == 1
    outer = (blk + near) % 2 == 0
    across = (blk + high) % n_blk
    along = blk + 1 - 2 * (blk % 2)
    core_id = (blk, near * 2 + other(core))
    near_id = (blk, other(near) * 2 + core)
    across_id = (across, rep)
    along_id = (along, rep)
    touch_id = (along, other(near) * 2 + core)

    barrier = pltpu.get_barrier_semaphore()
    for partner in (core_id, near_id, across_id, along_id, touch_id):
        pl.semaphore_signal(barrier, inc=1, device_id=partner, device_id_type=MESH)

    def part_of(d):
        return ((near + d // 2) % 2) * 2 + (core + d % 2) % 2

    def count_copy(rnd, d):
        start = pl.multiple_of(part_of(d) * local, local)
        return pltpu.make_async_copy(
            counts_ref.at[rnd, :, pl.ds(start, local)], counts.at[rnd * PARTS + d], count_sem.at[rnd * PARTS + d]
        )

    for rnd in range(rounds):
        for d in range(PARTS):
            count_copy(rnd, d).start()

    def send(kind, g, src, dst, sem, target):
        pltpu.make_async_remote_copy(
            src_ref=src, dst_ref=dst, send_sem=send_sem.at[kind, g], recv_sem=sem, device_id=target, device_id_type=MESH
        ).start()

    def landed(ref, sem):
        pltpu.make_async_copy(ref, ref, sem).wait()

    def lanes(j):
        return pl.ds(pl.multiple_of(j * piece, piece), piece)

    cols_f[width:, :] = jnp.zeros((padded - width, local), jnp.float32)
    cols_f[:width, :] = cols_ref[...]
    rows_f[width:, :] = jnp.zeros((padded - width, local), jnp.float32)
    rows_f[:width, :] = rows_ref[...]

    def send_cols(g, rnd):
        sent[g] = cols_f[:, lanes(g % cuts)].astype(jnp.bfloat16)

    for j in range(cuts):
        sent[j] = cols_f[:, j * piece : (j + 1) * piece].astype(jnp.bfloat16)
    pl.semaphore_wait(barrier, 5)
    for j in range(cuts):
        send(TO_PARTNER, j, sent.at[j], came.at[0, j], came_sem.at[0, j], across_id)

    def set_rows():
        rows = rows_f[...]
        rows_t[...] = rows.astype(jnp.bfloat16)
        rows_n[...] = rows.T.astype(jnp.bfloat16)
        row_grad[...] = jnp.zeros_like(row_grad)

    set_rows()
    margins = margin_ref[...]
    most = jnp.max(jnp.max(margins, axis=0, keepdims=True), axis=1, keepdims=True)
    mass = jnp.sum(jnp.sum(jnp.exp(margins - most), axis=0, keepdims=True), axis=1, keepdims=True)
    log_total = jnp.log(mass) + most
    lines = local // 128
    for k in range(lines):
        line = margin_ref[pl.ds((blk * PARTS + rep) * lines + k, 1), :]
        row_margin[k * 128 : (k + 1) * 128, :] = jnp.broadcast_to(line, (128, 128)).T - log_total

    scale = float(1.0 / (PARTS * local) ** 0.5)

    def prepare(g, d):
        rnd, j = g // cuts, g % cuts
        partner = across + rnd * (along - across)
        first = (partner * PARTS + part_of(d)) * lines + j * (piece // 128)

        @pl.when(j == 0)
        def _():
            count_copy(rnd, d).wait()

        for h in range(piece // 128):
            number = counts[rnd * PARTS + d, :, pl.ds(pl.multiple_of(j * piece + h * 128, 128), 128)]
            count = number.astype(jnp.float32)
            least = jnp.maximum(count, 1.0)
            confidence = scale * 0.1 + (scale * 0.25) * (count * lax.rsqrt(least))
            gain[g * PARTS + d, :, h * 128 : (h + 1) * 128] = jnp.where(number > 0, confidence, -0.5)
            shift[g * PARTS + d, :, h * 128 : (h + 1) * 128] = (
                row_margin[...] + margin_ref[pl.ds(first + h, 1), :]
            ) - jnp.log(least)

    def compute(g, d):
        block = came[d, g]
        pred = jnp.dot(rows_n[...], block, preferred_element_type=jnp.float32)
        factor = gain[g * PARTS + d]
        value = factor * (pred + shift[g * PARTS + d])
        smooth = (0.5 * scale) - (0.5 * scale) * jnp.tanh(value)
        slope = jnp.where(factor > 0.0, value, smooth).astype(jnp.bfloat16)
        far = jnp.dot(rows_t[...], slope, preferred_element_type=jnp.float32)
        row_grad[...] += lax.dot_general(block, slope, (((1,), (1,)), ((), ())), preferred_element_type=jnp.float32)
        if d % 2 == 0:
            part_own[d // 2, g] = far
        else:
            part_out[d // 2, g] = far.astype(jnp.bfloat16)
            send(PART_A + d // 2, g, part_out.at[d // 2, g], part_in.at[d // 2, g], part_sem.at[d // 2, g], core_id)

    def pass_first(g):
        landed(came.at[0, g], came_sem.at[0, g])
        send(TO_CORE, g, came.at[0, g], came.at[1, g], came_sem.at[1, g], core_id)

        @pl.when((g < cuts) | inner)
        def _():
            send(TO_NEAR, g, came.at[0, g], came.at[2, g], came_sem.at[2, g], near_id)

    def pass_second(g):
        landed(came.at[2, g], came_sem.at[2, g])
        send(TO_CORE_FAR, g, came.at[2, g], came.at[3, g], came_sem.at[3, g], core_id)

        @pl.when((g >= cuts) & inner)
        def _():
            send(TO_NEAR_FAR, g, came.at[2, g], came.at[0, g], came_sem.at[0, g], near_id)

    def chip_sum(g, k):
        landed(part_in.at[k, g], part_sem.at[k, g])
        return part_own[k, g] + part_in[k, g].astype(jnp.float32)

    def reduce_near(g):
        @pl.when((g < cuts) | outer)
        def _():
            near_out[0, g] = chip_sum(g, 1).astype(jnp.bfloat16)
            send(SUM_NEAR, g, near_out.at[0, g], near_in.at[0, g], near_sem.at[0, g], near_id)

        @pl.when((g >= cuts) & outer)
        def _():
            near_out[1, g] = chip_sum(g, 0).astype(jnp.bfloat16)
            send(SUM_NEAR_FAR, g, near_out.at[1, g], near_in.at[1, g], near_sem.at[1, g], near_id)

    def both_sum(g, k):
        own = chip_sum(g, k)
        landed(near_in.at[k, g], near_sem.at[k, g])
        return (own + near_in[k, g].astype(jnp.float32)).astype(jnp.bfloat16)

    def reduce_far(g):
        rnd = g // cuts

        @pl.when((g < cuts) | inner)
        def _():
            total_out[0, g] = both_sum(g, 0)
            send(
                TOTAL, g, total_out.at[0, g], total_in.at[g], total_sem.at[g], (across + rnd * (along - across), rep)
            )

        @pl.when((g >= cuts) & inner)
        def _():
            total_out[1, g] = both_sum(g, 1)
            send(TOTAL_FAR, g, total_out.at[1, g], total_in.at[g], total_sem.at[g], touch_id)

    def finish(g):
        j = g % cuts
        landed(total_in.at[g], total_sem.at[g])
        new = cols_f[:, lanes(j)] - STEP * total_in[g].astype(jnp.float32)
        cols_f[:, lanes(j)] = new

        @pl.when(g < pieces - cuts)
        def _():
            later = g + cuts
            sent[later] = new.astype(jnp.bfloat16)

            @pl.when(outer)
            def _():
                send(TO_PARTNER, later, sent.at[later], came.at[0, later], came_sem.at[0, later], along_id)

            @pl.when(inner)
            def _():
                send(TO_PARTNER, later, sent.at[later], came.at[2, later], came_sem.at[2, later], touch_id)

    pass_first(0)
    for d in range(PARTS):
        prepare(0, d)
    pass_second(0)

    def body(g, carry):
        @pl.when(g == cuts)
        def _():
            rows_f[...] = rows_f[...] - STEP * row_grad[...]
            set_rows()

        for d in range(PARTS):
            @pl.when(g < pieces)
            def _():
                if d % 2 == 1:
                    landed(came.at[d, g], came_sem.at[d, g])
                compute(g, d)

            if d == 1:
                @pl.when((g >= 1) & (g <= pieces))
                def _():
                    reduce_near(g - 1)

                @pl.when(g + 1 < cuts)
                def _():
                    pass_first(g + 1)

            @pl.when(g + 1 < pieces)
            def _():
                prepare(g + 1, d)

        @pl.when(g + 1 < cuts)
        def _():
            pass_second(g + 1)

        @pl.when((g >= 1) & (g <= pieces))
        def _():
            reduce_far(g - 1)

        @pl.when(g >= 2)
        def _():
            finish(g - 2)

        @pl.when((g + 1 >= cuts) & (g + 1 < pieces))
        def _():
            pass_first(g + 1)
            pass_second(g + 1)

        return carry

    lax.fori_loop(0, pieces + 2, body, 0)

    rows_out[...] = rows_f[:width, :] - STEP * row_grad[:width, :]
    cols_out[...] = cols_f[:width, :]

    def sent_off(g, carry):
        def wait(kind):
            pltpu.make_async_copy(sent.at[g], sent.at[g], send_sem.at[kind, g]).wait()

        for kind in (TO_PARTNER, TO_CORE, TO_CORE_FAR, PART_A, PART_B):
            wait(kind)

        @pl.when((g < cuts) | inner)
        def _():
            wait(TO_NEAR)
            wait(TOTAL)

        @pl.when((g >= cuts) & inner)
        def _():
            wait(TO_NEAR_FAR)
            wait(TOTAL_FAR)

        @pl.when((g < cuts) | outer)
        def _():
            wait(SUM_NEAR)

        @pl.when((g >= cuts) & outer)
        def _():
            wait(SUM_NEAR_FAR)

        return carry

    lax.fori_loop(0, pieces, sent_off, 0)


def solution(mesh):
    n_blk = mesh.shape["blk"]

    def per_device(row_embed, col_embed, counts, log_marginal):
        local, width = row_embed.shape
        rounds = counts.shape[0]
        padded = -(-width // 16) * 16
        piece = local // CUTS
        pieces = rounds * CUTS
        vmem = pltpu.VMEM
        f32, half = jnp.float32, jnp.bfloat16
        block = (padded, piece)
        rows_t, cols_t = pl.pallas_call(
            functools.partial(kernel, n_blk, rounds, CUTS, piece),
            out_shape=[jax.ShapeDtypeStruct((width, local), f32)] * 2,
            in_specs=[
                pl.BlockSpec(memory_space=vmem),
                pl.BlockSpec(memory_space=vmem),
                pl.BlockSpec(memory_space=pl.ANY),
                pl.BlockSpec(memory_space=vmem),
            ],
            out_specs=[pl.BlockSpec(memory_space=vmem)] * 2,
            scratch_shapes=[
                vmem((rounds * PARTS, local, local), jnp.int32),
                vmem((pieces * PARTS, local, piece), f32),
                vmem((pieces * PARTS, local, piece), f32),
                vmem((padded, local), f32),
                vmem((padded, local), half),
                vmem((local, padded), half),
                vmem((padded, local), f32),
                vmem((padded, local), f32),
                vmem((local, 128), f32),
                vmem((pieces,) + block, half),
                vmem((PARTS, pieces) + block, half),
                vmem((2, pieces) + block, f32),
                vmem((2, pieces) + block, half),
                vmem((2, pieces) + block, half),
                vmem((2, pieces) + block, half),
                vmem((2, pieces) + block, half),
                vmem((2, pieces) + block, half),
                vmem((pieces,) + block, half),
                pltpu.SemaphoreType.DMA((rounds * PARTS,)),
                pltpu.SemaphoreType.DMA((KINDS, pieces)),
                pltpu.SemaphoreType.DMA((PARTS, pieces)),
                pltpu.SemaphoreType.DMA((2, pieces)),
                pltpu.SemaphoreType.DMA((2, pieces)),
                pltpu.SemaphoreType.DMA((pieces,)),
            ],
            compiler_params=pltpu.CompilerParams(
                collective_id=0, has_side_effects=True, vmem_limit_bytes=60 * 2**20
            ),
        )(row_embed.T, col_embed.T, counts, log_marginal.reshape(-1, 128))
        return rows_t.T, cols_t.T

    placed = (P(("blk", "rep"), None), P(("blk", "rep"), None), P(None, ("blk", "rep"), None), P())
    return jax.shard_map(
        per_device,
        mesh=mesh,
        in_specs=placed,
        out_specs=(P(("blk", "rep"), None), P(("blk", "rep"), None)),
        check_vma=False,
    )
```

time: 298 us -> 99.9 us (0.34)
  waiting for transfers between devices: 236 us -> 0 us
  Pallas kernels: 0 us -> 94.9 us
  matrix products: 23.6 us -> 0 us
  between operations: 15.8 us -> 0.64 us
  starting transfers between devices: 11.2 us -> 0 us
  other arithmetic: 8.08 us -> 0 us
    ppermute x4 -> x0, waiting for transfers between devices: 113 us -> none  [swapped(): return lax.ppermute(value, axis, pairs)]
    pallas_call x0 -> x1, Pallas kernels: none -> 94.9 us  [per_device(): pl.pallas_call(functools.partial(kernel, n_blk, rounds, CUTS, piece), out...]
    reduce_scatter x2 -> x0, waiting for transfers between devices: 69.2 us -> none  [fit_round(): summed = lax.psum_scatter(far_grad, 'rep', scatter_dimension=0, tiled=True)]
    all_gather x2 -> x0, waiting for transfers between devices: 54 us -> none  [fit_round(): whole_block = lax.all_gather(col_half, 'rep', axis=0, tiled=True)]
    dot_general x6 -> x0, matrix products: 23.6 us -> none  [the longest x2 13.4 us: fit_round(): lax.dot_general(row_half, partner_cols, (((1,), (1,)), ((), ())), preferr...]
    ppermute x4 -> x0, starting transfers between devices: 11.1 us -> none  [swapped(): return lax.ppermute(value, axis, pairs)]
  transfers between devices with their start and end apart: 8 -> 0, of which waited for: 8 -> 0; matrix products, arithmetic and copies ran while one was open for 4% -> 0% of each run, Pallas kernels for 0% -> 0%
where the time goes in v1:
time: 99.9 us; the launch traced here: 99.4 us
  Pallas kernels  94.9 us (95%)
  local copies, waits for them, and re-layouts  3.88 us (4%)
    pallas_call x1, Pallas kernels, per_device(): pl.pallas_call(functools.partial(kernel, n_blk, rounds, CUTS, piece), out...  94.9 us
    unnamed x2, local copies, waits for them, and re-layouts  3.88 us

profile of v1, /device:TPU:16, one launch (start us, length us, event | category | flops | bytes accessed | tf_op | source)
XLA Modules:
  0.0 99.4 jit_solution(12975740634304397747)
XLA Ops:
  0.6 94.9 %shard_map.59 = (f32[300,512]{1,0:T(8,128)}, f32[300,512]{1,0:T(8,128)}) custom-call(f32[300,512]{1,0:T(8,128)} %bitcast.5, f32[300,512]{1,0:T(8,128)} %bitcast.6, s32[2,512,2048]{2,1,0:T(8,128)} %counts_ref.1, f32[1024,128]{1,0:T(8,128)} %bitcast.9), custom_call_target="tpu_custom_call" | custom-call | tf_op jit(solution)/shard_map/pallas_call | solution.py:308
  95.5 1.9 %copy.8 = f32[512,300]{0,1:T(8,128)} copy(f32[512,300]{0,1:T(8,128)} %bitcast.8) | data formatting | bytes 1228800
  97.5 1.9 %copy.9 = f32[512,300]{0,1:T(8,128)} copy(f32[512,300]{0,1:T(8,128)} %bitcast.7) | data formatting | bytes 1228800

commit v2 on v1

v2 whole, which is shorter than its diff:
```python
import functools

import jax
import jax.numpy as jnp
from jax import lax
from jax.experimental import pallas as pl
from jax.experimental.pallas import tpu as pltpu
from jax.sharding import PartitionSpec as P

STEP = 0.05
PARTS = 4
CUTS = 4
MESH = pl.DeviceIdType.MESH
TO_PARTNER, TO_CORE, TO_NEAR, TO_CORE_FAR, PART_A, PART_B, SUM_NEAR, SUM_NEAR_FAR, TOTAL, TOTAL_FAR, TO_NEAR_FAR = range(11)
KINDS = 11


def other(bit):
    return 1 - bit


def kernel(
    n_blk, rounds, cuts, piece,
    rows_ref, cols_ref, counts_ref, margin_hbm, rows_out, cols_out,
    counts, gain, shift, rows_f, rows_t, rows_n, row_grad, cols_f, row_margin,
    sent, came, part_own, part_out, part_in, near_out, near_in, total_out, total_in,
    margin_ref, rows_in, cols_in, load_sem, count_sem, send_sem, came_sem, part_sem, near_sem, total_sem,
):
    width, local = rows_ref.shape
    padded = rows_f.shape[0]
    pieces = rounds * cuts
    units = 2 * cuts
    blk = lax.axis_index("blk")
    rep = lax.axis_index("rep")
    near = rep // 2
    core = rep % 2
    far_rep = other(near) * 2 + core
    inner = (blk + near) % 2 == 1
    outer = (blk + near) % 2 == 0
    across = (blk + n_blk // 2) % n_blk
    along = blk + 1 - 2 * (blk % 2)
    both = across + 1 - 2 * (across % 2)
    core_id = (blk, near * 2 + other(core))
    near_id = (blk, far_rep)
    across_id = (across, rep)
    along_id = (along, rep)
    touch_id = (along, far_rep)
    both_along_id = (both, rep)
    both_touch_id = (both, far_rep)
    partners = (core_id, near_id, across_id, along_id)

    barrier = pltpu.get_barrier_semaphore()
    for partner in partners:
        pl.semaphore_signal(barrier, inc=1, device_id=partner, device_id_type=MESH)

    def part_of(d):
        return ((near + d // 2) % 2) * 2 + (core + d % 2) % 2

    def count_copy(rnd, d):
        start = pl.multiple_of(part_of(d) * local, local)
        return pltpu.make_async_copy(
            counts_ref.at[rnd, :, pl.ds(start, local)], counts.at[rnd * PARTS + d], count_sem.at[rnd * PARTS + d]
        )

    loads = [
        pltpu.make_async_copy(cols_ref, cols_in, load_sem.at[0]),
        pltpu.make_async_copy(rows_ref, rows_in, load_sem.at[1]),
        pltpu.make_async_copy(margin_hbm, margin_ref, load_sem.at[2]),
    ]
    for load in loads:
        load.start()
    for rnd in range(rounds):
        for d in range(PARTS):
            count_copy(rnd, d).start()

    def send(kind, g, src, dst, sem, target):
        pltpu.make_async_remote_copy(
            src_ref=src, dst_ref=dst, send_sem=send_sem.at[kind, g], recv_sem=sem, device_id=target, device_id_type=MESH
        ).start()

    def landed(ref, sem):
        pltpu.make_async_copy(ref, ref, sem).wait()

    def lanes(j):
        return pl.ds(pl.multiple_of(j * piece, piece), piece)

    cols_f[width:, :] = jnp.zeros((padded - width, local), jnp.float32)
    rows_f[width:, :] = jnp.zeros((padded - width, local), jnp.float32)
    loads[0].wait()
    cols_f[:width, :] = cols_in[...]
    for j in range(cuts):
        sent[j] = cols_f[:, j * piece : (j + 1) * piece].astype(jnp.bfloat16)
    pl.semaphore_wait(barrier, len(partners))
    for j in range(cuts):
        send(TO_PARTNER, j, sent.at[j], came.at[0, j], came_sem.at[0, j], across_id)

    loads[1].wait()
    rows_f[:width, :] = rows_in[...]

    def set_rows():
        rows = rows_f[...]
        rows_t[...] = rows.astype(jnp.bfloat16)
        rows_n[...] = rows.T.astype(jnp.bfloat16)
        row_grad[...] = jnp.zeros_like(row_grad)

    set_rows()
    loads[2].wait()
    margins = margin_ref[...]
    most = jnp.max(jnp.max(margins, axis=0, keepdims=True), axis=1, keepdims=True)
    mass = jnp.sum(jnp.sum(jnp.exp(margins - most), axis=0, keepdims=True), axis=1, keepdims=True)
    log_total = jnp.log(mass) + most
    lines = local // 128
    for k in range(lines):
        line = margin_ref[pl.ds((blk * PARTS + rep) * lines + k, 1), :]
        row_margin[k * 128 : (k + 1) * 128, :] = jnp.broadcast_to(line, (128, 128)).T - log_total

    scale = float(1.0 / (PARTS * local) ** 0.5)

    def prepare(g, k):
        rnd, j = g // cuts, g % cuts
        partner = across + rnd * (along - across)

        @pl.when(j == 0)
        def _():
            for h in range(2):
                count_copy(rnd, 2 * k + h).wait()

        for h in range(2):
            d = 2 * k + h
            first = (partner * PARTS + part_of(d)) * lines + j
            number = counts[rnd * PARTS + d, :, lanes(j)]
            count = number.astype(jnp.float32)
            least = jnp.maximum(count, 1.0)
            confidence = scale * 0.1 + (scale * 0.25) * (count * lax.rsqrt(least))
            gain[g * 2 + k, :, h * piece : (h + 1) * piece] = jnp.where(number > 0, confidence, -0.5)
            shift[g * 2 + k, :, h * piece : (h + 1) * piece] = (
                row_margin[...] + margin_ref[pl.ds(first, 1), :]
            ) - jnp.log(least)

    def compute(g, k):
        block = jnp.concatenate([came[2 * k, g], came[2 * k + 1, g]], axis=1)
        pred = jnp.dot(rows_n[...], block, preferred_element_type=jnp.float32)
        factor = gain[g * 2 + k]
        value = factor * (pred + shift[g * 2 + k])
        smooth = (0.5 * scale) - (0.5 * scale) * jnp.tanh(value)
        slope = jnp.where(factor > 0.0, value, smooth).astype(jnp.bfloat16)
        far = jnp.dot(rows_t[...], slope, preferred_element_type=jnp.float32)
        part_own[k, g] = far[:, :piece]
        part_out[k, g] = far[:, piece:]
        send(PART_A + k, g, part_out.at[k, g], part_in.at[k, g], part_sem.at[k, g], core_id)
        row_grad[...] += lax.dot_general(block, slope, (((1,), (1,)), ((), ())), preferred_element_type=jnp.float32)

    def arrived(d, g):
        landed(came.at[d, g], came_sem.at[d, g])

    def pass_first(g):
        arrived(0, g)
        send(TO_CORE, g, came.at[0, g], came.at[1, g], came_sem.at[1, g], core_id)

        def on():
            send(TO_NEAR, g, came.at[0, g], came.at[2, g], came_sem.at[2, g], near_id)

        on() if g < cuts else pl.when(inner)(on)

    def pass_second(g):
        arrived(2, g)
        send(TO_CORE_FAR, g, came.at[2, g], came.at[3, g], came_sem.at[3, g], core_id)
        if g >= cuts:
            @pl.when(inner)
            def _():
                send(TO_NEAR_FAR, g, came.at[2, g], came.at[0, g], came_sem.at[0, g], near_id)

    def chip_sum(g, k):
        landed(part_in.at[k, g], part_sem.at[k, g])
        return part_own[k, g] + part_in[k, g]

    def to_near(g, k):
        near_out[1 - k, g] = chip_sum(g, k).astype(jnp.bfloat16)
        send(SUM_NEAR + 1 - k, g, near_out.at[1 - k, g], near_in.at[1 - k, g], near_sem.at[1 - k, g], near_id)

    def both_sum(g, k):
        own = chip_sum(g, k)
        landed(near_in.at[k, g], near_sem.at[k, g])
        return own + near_in[k, g].astype(jnp.float32)

    def total_first(g):
        later = g + cuts
        total = both_sum(g, 0)
        sent[later] = (came[0, g].astype(jnp.float32) - STEP * total).astype(jnp.bfloat16)

        @pl.when(outer)
        def _():
            send(TO_PARTNER, later, sent.at[later], came.at[0, later], came_sem.at[0, later], both_along_id)

        @pl.when(inner)
        def _():
            send(TO_PARTNER, later, sent.at[later], came.at[2, later], came_sem.at[2, later], both_touch_id)

        total_out[0, g] = total.astype(jnp.bfloat16)
        send(TOTAL, g, total_out.at[0, g], total_in.at[g], total_sem.at[g], across_id)

    def total_last(g):
        total_out[0, g] = both_sum(g, 0).astype(jnp.bfloat16)
        send(TOTAL, g, total_out.at[0, g], total_in.at[g], total_sem.at[g], along_id)
        total_out[1, g] = both_sum(g, 1).astype(jnp.bfloat16)
        send(TOTAL_FAR, g, total_out.at[1, g], total_in.at[g], total_sem.at[g], touch_id)

    def finish(g):
        j = g % cuts
        landed(total_in.at[g], total_sem.at[g])
        spot = slice(j * piece, (j + 1) * piece)
        cols_f[:, spot] = cols_f[:, spot] - STEP * total_in[g].astype(jnp.float32)

    def new_rows():
        rows_f[...] = rows_f[...] - STEP * row_grad[...]
        set_rows()

    def ready(s, carry):
        prepare(s // 2, s % 2)
        return carry

    lax.fori_loop(0, units, ready, 0)

    def ready_more(low, high):
        lax.fori_loop(units + low, units + high, ready, 0)

    ahead = [
        [(pass_first, 0), (arrived, 1, 0)],
        [(pass_first, 1), (arrived, 1, 1)],
        [(pass_first, 2), (pass_second, 0), (arrived, 3, 0)],
        [(arrived, 1, 2)],
        [(pass_first, 3), (pass_second, 1), (arrived, 3, 1)],
        [(arrived, 1, 3)],
        [(to_near, 0, 1), (pass_second, 2), (arrived, 3, 2)],
        [(to_near, 1, 1), (pass_second, 3), (arrived, 3, 3)],
        [
            (to_near, 2, 1), (total_first, 0), (to_near, 3, 1), (new_rows,), (total_first, 1), (ready_more, 0, 3),
            (total_first, 2), (ready_more, 3, 6), (total_first, 3), (ready_more, 6, 8), (pass_first, 4), (pass_second, 4),
            (arrived, 1, 4),
        ],
        [(arrived, 3, 4)],
    ]
    for g in range(cuts + 1, pieces):
        ahead.append(["outer", (to_near, g - 1, 0), (to_near, g - 1, 1), "all", (pass_first, g), (pass_second, g), (arrived, 1, g)])
        if g == cuts + 2:
            ahead[-1] += [(finish, 0), (finish, 1)]
        if g == cuts + 3:
            ahead[-1] += [(finish, 2), (finish, 3)]
        ahead.append([(arrived, 3, g)])

    def act(steps):
        mine, rest = [], []
        for step in steps:
            if step == "outer":
                rest = mine
                mine = []
            elif step == "all":
                todo = mine

                @pl.when(outer)
                def _():
                    for call, *args in todo:
                        call(*args)

                mine = []
            else:
                mine.append(step)
        for call, *args in mine:
            call(*args)

    def body(t, carry):
        rnd, s = t // units, t % units
        k0 = other(s % 2) * ((s + units - 1) // units) + s // (units - 1)
        j0 = (s + 1) // 2 - k0
        j = j0 + rnd * (s // 2 - j0)
        k = k0 + rnd * (s % 2 - k0)
        g = rnd * cuts + j

        for start in range(0, len(ahead), 4):
            @pl.when((t >= start) & (t < start + 4))
            def _():
                for now in range(start, start + 4):
                    pl.when(t == now)(functools.partial(act, ahead[now]))

        compute(g, k)
        return carry

    lax.fori_loop(0, rounds * units, body, 0)

    @pl.when(outer)
    def _():
        to_near(pieces - 1, 0)
        to_near(pieces - 1, 1)

    rows_out[...] = rows_f[:width, :] - STEP * row_grad[:width, :]

    @pl.when(inner)
    def _():
        for g in range(cuts, pieces):
            total_last(g)

    for g in range(cuts, pieces):
        finish(g)
    cols_out[...] = cols_f[:width, :]

    def sent_off(g, carry):
        def wait(kind, ref):
            pltpu.make_async_copy(ref, ref, send_sem.at[kind, g]).wait()

        for kind in (TO_PARTNER, TO_CORE, TO_CORE_FAR):
            wait(kind, sent.at[g])
        for kind in (PART_A, PART_B):
            wait(kind, part_out.at[0, g])

        @pl.when((g < cuts) | inner)
        def _():
            wait(TO_NEAR, sent.at[g])
            wait(TOTAL, sent.at[g])

        @pl.when((g >= cuts) & inner)
        def _():
            wait(TO_NEAR_FAR, sent.at[g])
            wait(TOTAL_FAR, sent.at[g])

        @pl.when((g < cuts) | outer)
        def _():
            wait(SUM_NEAR, sent.at[g])

        @pl.when((g >= cuts) & outer)
        def _():
            wait(SUM_NEAR_FAR, sent.at[g])

        return carry

    lax.fori_loop(0, pieces, sent_off, 0)


def settle(rows_ref, cols_ref, rows_out, cols_out, sem):
    copies = [
        pltpu.make_async_copy(rows_ref, rows_out, sem.at[0]),
        pltpu.make_async_copy(cols_ref, cols_out, sem.at[1]),
    ]
    for copy in copies:
        copy.start()
    for copy in copies:
        copy.wait()


def solution(mesh):
    n_blk = mesh.shape["blk"]

    def per_device(row_embed, col_embed, counts, log_marginal):
        local, width = row_embed.shape
        rounds = counts.shape[0]
        padded = -(-width // 16) * 16
        piece = local // CUTS
        pieces = rounds * CUTS
        vmem = pltpu.VMEM
        f32, half = jnp.float32, jnp.bfloat16
        block = (padded, piece)
        rows_t, cols_t = pl.pallas_call(
            functools.partial(kernel, n_blk, rounds, CUTS, piece),
            out_shape=[jax.ShapeDtypeStruct((width, local), f32)] * 2,
            in_specs=[
                pl.BlockSpec(memory_space=pl.ANY),
                pl.BlockSpec(memory_space=pl.ANY),
                pl.BlockSpec(memory_space=pl.ANY),
                pl.BlockSpec(memory_space=pl.ANY),
            ],
            out_specs=[pl.BlockSpec(memory_space=vmem)] * 2,
            scratch_shapes=[
                vmem((rounds * PARTS, local, local), jnp.int32),
                vmem((pieces * 2, local, 2 * piece), f32),
                vmem((pieces * 2, local, 2 * piece), f32),
                vmem((padded, local), f32),
                vmem((padded, local), half),
                vmem((local, padded), half),
                vmem((padded, local), f32),
                vmem((padded, local), f32),
                vmem((local, 128), f32),
                vmem((pieces,) + block, half),
                vmem((PARTS, pieces) + block, half),
                vmem((2, pieces) + block, f32),
                vmem((2, pieces) + block, f32),
                vmem((2, pieces) + block, f32),
                vmem((2, pieces) + block, half),
                vmem((2, pieces) + block, half),
                vmem((2, pieces) + block, half),
                vmem((pieces,) + block, half),
                vmem((local * PARTS * n_blk // 128, 128), f32),
                vmem((width, local), f32),
                vmem((width, local), f32),
                pltpu.SemaphoreType.DMA((3,)),
                pltpu.SemaphoreType.DMA((rounds * PARTS,)),
                pltpu.SemaphoreType.DMA((KINDS, pieces)),
                pltpu.SemaphoreType.DMA((PARTS, pieces)),
                pltpu.SemaphoreType.DMA((2, pieces)),
                pltpu.SemaphoreType.DMA((2, pieces)),
                pltpu.SemaphoreType.DMA((pieces,)),
            ],
            compiler_params=pltpu.CompilerParams(
                collective_id=0, has_side_effects=True, vmem_limit_bytes=52 * 2**20
            ),
        )(row_embed.T, col_embed.T, counts, log_marginal.reshape(-1, 128))
        rows_t, cols_t = pl.pallas_call(
            settle,
            out_shape=[jax.ShapeDtypeStruct((width, local), f32)] * 2,
            in_specs=[pl.BlockSpec(memory_space=pl.ANY)] * 2,
            out_specs=[pl.BlockSpec(memory_space=pl.ANY)] * 2,
            scratch_shapes=[pltpu.SemaphoreType.DMA((2,))],
            compiler_params=pltpu.CompilerParams(vmem_limit_bytes=2**20),
        )(rows_t, cols_t)
        return rows_t.T, cols_t.T

    placed = (P(("blk", "rep"), None), P(("blk", "rep"), None), P(None, ("blk", "rep"), None), P())
    return jax.shard_map(
        per_device,
        mesh=mesh,
        in_specs=placed,
        out_specs=(P(("blk", "rep"), None), P(("blk", "rep"), None)),
        check_vma=False,
    )
```

time: 99.9 us -> 66.8 us (0.67)
  Pallas kernels: 94.9 us -> 65 us
  local copies, waits for them, and re-layouts: 3.88 us -> 1.03 us
    pallas_call x1, Pallas kernels: 94.9 us -> 64 us  [per_device(): pl.pallas_call(functools.partial(kernel, n_blk, rounds, CUTS, piece), out...]
    unnamed x2, local copies, waits for them, and re-layouts: 3.88 us -> 1.03 us
    pallas_call x0 -> x1, Pallas kernels: none -> 1.05 us  [per_device(): pl.pallas_call(settle, out_shape=[jax.ShapeDtypeStruct((width, local), f3...]
where the time goes in v2:
time: 66.8 us; the launch traced here: 66.7 us
  Pallas kernels  65 us (97%)
  local copies, waits for them, and re-layouts  1.03 us (2%)
    pallas_call x1, Pallas kernels, per_device(): pl.pallas_call(functools.partial(kernel, n_blk, rounds, CUTS, piece), out...  64 us

profile of v2, /device:TPU:16, one launch (start us, length us, event | category | flops | bytes accessed | tf_op | source)
XLA Modules:
  0.0 66.7 jit_solution(15690896997333436310)
XLA Ops:
  0.6 0.0 copy-start
  0.6 1.0 %copy-done = f32[131072]{0:T(1024)S(1)} copy-done((f32[131072]{0:T(1024)S(1)}, f32[131072]{0:T(1024)}, u32[]{:S(2)}) %copy-start) | copy-done | bytes 524312
  1.7 64.0 %shard_map.59 = (f32[300,512]{1,0:T(8,128)S(1)}, f32[300,512]{1,0:T(8,128)S(1)}) custom-call(f32[300,512]{1,0:T(8,128)} %bitcast.6, f32[300,512]{1,0:T(8,128)} %bitcast.7, s32[2,512,2048]{2,1,0:T(8,128)} %counts_ref.1, f32[1024,128]{1,0:T(8,128)S(1)} %bitcast.5), custom_call_target="tpu_custom_call" | custom-call | tf_op jit(solution)/shard_map/pallas_call | solution.py:361
  65.7 1.1 %shard_map.60 = (f32[300,512]{1,0:T(8,128)}, f32[300,512]{1,0:T(8,128)}) custom-call(f32[300,512]{1,0:T(8,128)S(1)} %get-tuple-element.6.rows_ref, f32[300,512]{1,0:T(8,128)S(1)} %get-tuple-element.7.cols_ref), custom_call_target="tpu_custom_call" | custom-call | tf_op jit(solution)/shard_map/pallas_call | solution.py:405
Async XLA Ops:
  0.6 1.0 %copy-start = (f32[131072]{0:T(1024)S(1)}, f32[131072]{0:T(1024)}, u32[]{:S(2)}) copy-start(f32[131072]{0:T(1024)} %param.7) | copy-start | bytes 1572868

commit v3 on v2

--- a/solution.py
+++ b/solution.py
@@ -75,7 +75,7 @@
 
     def send(kind, g, src, dst, sem, target):
         pltpu.make_async_remote_copy(
-            src_ref=src, dst_ref=dst, send_sem=send_sem.at[kind, g], recv_sem=sem, device_id=target, device_id_type=MESH
+            src_ref=src, dst_ref=dst, send_sem=send_sem.at[kind], recv_sem=sem, device_id=target, device_id_type=MESH
         ).start()
 
     def landed(ref, sem):
@@ -139,11 +139,16 @@
 
     def compute(g, k):
         block = jnp.concatenate([came[2 * k, g], came[2 * k + 1, g]], axis=1)
-        pred = jnp.dot(rows_n[...], block, preferred_element_type=jnp.float32)
-        factor = gain[g * 2 + k]
-        value = factor * (pred + shift[g * 2 + k])
-        smooth = (0.5 * scale) - (0.5 * scale) * jnp.tanh(value)
-        slope = jnp.where(factor > 0.0, value, smooth).astype(jnp.bfloat16)
+        slopes = []
+        height = local // 4
+        for part in range(4):
+            span = slice(part * height, (part + 1) * height)
+            pred = jnp.dot(rows_n[span, :], block, preferred_element_type=jnp.float32)
+            factor = gain[g * 2 + k, span, :]
+            value = factor * (pred + shift[g * 2 + k, span, :])
+            smooth = (0.5 * scale) - (0.5 * scale) * jnp.tanh(value)
+            slopes.append(jnp.where(factor > 0.0, value, smooth).astype(jnp.bfloat16))
+        slope = jnp.concatenate(slopes, axis=0)
         far = jnp.dot(rows_t[...], slope, preferred_element_type=jnp.float32)
         part_own[k, g] = far[:, :piece]
         part_out[k, g] = far[:, piece:]
@@ -209,7 +214,11 @@
         j = g % cuts
         landed(total_in.at[g], total_sem.at[g])
         spot = slice(j * piece, (j + 1) * piece)
-        cols_f[:, spot] = cols_f[:, spot] - STEP * total_in[g].astype(jnp.float32)
+        new = cols_f[:, spot] - STEP * total_in[g].astype(jnp.float32)
+        if g < pieces - cuts:
+            cols_f[:, spot] = new
+        else:
+            cols_out[:, spot] = new[:width, :]
 
     def new_rows():
         rows_f[...] = rows_f[...] - STEP * row_grad[...]
@@ -232,16 +241,16 @@
         [(pass_first, 3), (pass_second, 1), (arrived, 3, 1)],
         [(arrived, 1, 3)],
         [(to_near, 0, 1), (pass_second, 2), (arrived, 3, 2)],
-        [(to_near, 1, 1), (pass_second, 3), (arrived, 3, 3)],
+        [(to_near, 1, 1), (total_first, 0), (pass_second, 3), (arrived, 3, 3)],
         [
-            (to_near, 2, 1), (total_first, 0), (to_near, 3, 1), (new_rows,), (total_first, 1), (ready_more, 0, 3),
+            (to_near, 2, 1), (to_near, 3, 1), (new_rows,), (total_first, 1), (ready_more, 0, 3),
             (total_first, 2), (ready_more, 3, 6), (total_first, 3), (ready_more, 6, 8), (pass_first, 4), (pass_second, 4),
             (arrived, 1, 4),
         ],
         [(arrived, 3, 4)],
     ]
     for g in range(cuts + 1, pieces):
-        ahead.append(["outer", (to_near, g - 1, 0), (to_near, g - 1, 1), "all", (pass_first, g), (pass_second, g), (arrived, 1, g)])
+        ahead.append(["outer", (to_near, g - 1, 1), (to_near, g - 1, 0), "all", (pass_first, g), (pass_second, g), (arrived, 1, g)])
         if g == cuts + 2:
             ahead[-1] += [(finish, 0), (finish, 1)]
         if g == cuts + 3:
@@ -289,8 +298,8 @@
 
     @pl.when(outer)
     def _():
+        to_near(pieces - 1, 1)
         to_near(pieces - 1, 0)
-        to_near(pieces - 1, 1)
 
     rows_out[...] = rows_f[:width, :] - STEP * row_grad[:width, :]
 
@@ -301,38 +310,25 @@
 
     for g in range(cuts, pieces):
         finish(g)
-    cols_out[...] = cols_f[:width, :]
-
-    def sent_off(g, carry):
-        def wait(kind, ref):
-            pltpu.make_async_copy(ref, ref, send_sem.at[kind, g]).wait()
-
-        for kind in (TO_PARTNER, TO_CORE, TO_CORE_FAR):
-            wait(kind, sent.at[g])
-        for kind in (PART_A, PART_B):
-            wait(kind, part_out.at[0, g])
-
-        @pl.when((g < cuts) | inner)
-        def _():
-            wait(TO_NEAR, sent.at[g])
-            wait(TOTAL, sent.at[g])
-
-        @pl.when((g >= cuts) & inner)
-        def _():
-            wait(TO_NEAR_FAR, sent.at[g])
-            wait(TOTAL_FAR, sent.at[g])
-
-        @pl.when((g < cuts) | outer)
-        def _():
-            wait(SUM_NEAR, sent.at[g])
-
-        @pl.when((g >= cuts) & outer)
-        def _():
-            wait(SUM_NEAR_FAR, sent.at[g])
-
-        return carry
-
-    lax.fori_loop(0, pieces, sent_off, 0)
+
+    def sent_off(kind, ref):
+        pltpu.make_async_copy(ref, ref, send_sem.at[kind]).wait()
+
+    half = sent.at[:cuts]
+    for kind in (TO_PARTNER, TO_CORE, TO_CORE_FAR):
+        sent_off(kind, sent)
+    for kind in (PART_A, PART_B):
+        sent_off(kind, part_out.at[0])
+
+    @pl.when(inner)
+    def _():
+        for kind, ref in ((TO_NEAR, sent), (TOTAL, sent), (TO_NEAR_FAR, half), (TOTAL_FAR, half), (SUM_NEAR, half)):
+            sent_off(kind, ref)
+
+    @pl.when(outer)
+    def _():
+        for kind, ref in ((TO_NEAR, half), (TOTAL, half), (SUM_NEAR, sent), (SUM_NEAR_FAR, half)):
+            sent_off(kind, ref)
 
 
 def settle(rows_ref, cols_ref, rows_out, cols_out, sem):
@@ -392,7 +388,7 @@
                 vmem((width, local), f32),
                 pltpu.SemaphoreType.DMA((3,)),
                 pltpu.SemaphoreType.DMA((rounds * PARTS,)),
-                pltpu.SemaphoreType.DMA((KINDS, pieces)),
+                pltpu.SemaphoreType.DMA((KINDS,)),
                 pltpu.SemaphoreType.DMA((PARTS, pieces)),
                 pltpu.SemaphoreType.DMA((2, pieces)),
                 pltpu.SemaphoreType.DMA((2, pieces)),

time: 66.8 us -> 63.9 us (0.957)
  Pallas kernels: 65 us -> 62.1 us
    pallas_call x1, Pallas kernels: 64 us -> 61.1 us  [per_device(): pl.pallas_call(functools.partial(kernel, n_blk, rounds, CUTS, piece), out...]
where the time goes in v3:
time: 63.9 us; the launch traced here: 63.8 us
  Pallas kernels  62.1 us (97%)
  local copies, waits for them, and re-layouts  1.03 us (2%)
  between operations  0.65 us (1%)
    pallas_call x1, Pallas kernels, per_device(): pl.pallas_call(functools.partial(kernel, n_blk, rounds, CUTS, piece), out...  61.1 us

profile of v3, /device:TPU:16, one launch (start us, length us, event | category | flops | bytes accessed | tf_op | source)
XLA Modules:
  0.0 63.8 jit_solution(15645719328708967388)
XLA Ops:
  0.6 0.0 copy-start
  0.6 1.0 %copy-done = f32[131072]{0:T(1024)S(1)} copy-done((f32[131072]{0:T(1024)S(1)}, f32[131072]{0:T(1024)}, u32[]{:S(2)}) %copy-start) | copy-done | bytes 524312
  1.7 61.1 %shard_map.59 = (f32[300,512]{1,0:T(8,128)S(1)}, f32[300,512]{1,0:T(8,128)S(1)}) custom-call(f32[300,512]{1,0:T(8,128)} %bitcast.6, f32[300,512]{1,0:T(8,128)} %bitcast.7, s32[2,512,2048]{2,1,0:T(8,128)} %counts_ref.1, f32[1024,128]{1,0:T(8,128)S(1)} %bitcast.5), custom_call_target="tpu_custom_call" | custom-call | tf_op jit(solution)/shard_map/pallas_call | solution.py:357
  62.8 1.1 %shard_map.60 = (f32[300,512]{1,0:T(8,128)}, f32[300,512]{1,0:T(8,128)}) custom-call(f32[300,512]{1,0:T(8,128)S(1)} %get-tuple-element.6.rows_ref, f32[300,512]{1,0:T(8,128)S(1)} %get-tuple-element.7.cols_ref), custom_call_target="tpu_custom_call" | custom-call | tf_op jit(solution)/shard_map/pallas_call | solution.py:401
Async XLA Ops:
  0.6 1.0 %copy-start = (f32[131072]{0:T(1024)S(1)}, f32[131072]{0:T(1024)}, u32[]{:S(2)}) copy-start(f32[131072]{0:T(1024)} %param.7) | copy-start | bytes 1572868

commit v4 on v3

--- a/solution.py
+++ b/solution.py
@@ -239,8 +239,8 @@
         [(pass_first, 2), (pass_second, 0), (arrived, 3, 0)],
         [(arrived, 1, 2)],
         [(pass_first, 3), (pass_second, 1), (arrived, 3, 1)],
-        [(arrived, 1, 3)],
-        [(to_near, 0, 1), (pass_second, 2), (arrived, 3, 2)],
+        [(to_near, 0, 1), (arrived, 1, 3)],
+        [(pass_second, 2), (arrived, 3, 2)],
         [(to_near, 1, 1), (total_first, 0), (pass_second, 3), (arrived, 3, 3)],
         [
             (to_near, 2, 1), (to_near, 3, 1), (new_rows,), (total_first, 1), (ready_more, 0, 3),

time: 63.9 us -> 63.3 us (level)
    pallas_call x1, Pallas kernels: 61.1 us -> 60.4 us  [per_device(): pl.pallas_call(functools.partial(kernel, n_blk, rounds, CUTS, piece), out...]
where the time goes in v4:
time: 63.3 us; the launch traced here: 63.1 us
  Pallas kernels  61.5 us (97%)
  local copies, waits for them, and re-layouts  1.03 us (2%)
  between operations  0.65 us (1%)
    pallas_call x1, Pallas kernels, per_device(): pl.pallas_call(functools.partial(kernel, n_blk, rounds, CUTS, piece), out...  60.4 us

profile of v4, /device:TPU:16, one launch (start us, length us, event | category | flops | bytes accessed | tf_op | source)
XLA Modules:
  0.0 63.1 jit_solution(9798565828763427047)
XLA Ops:
  0.6 0.0 copy-start
  0.6 1.0 %copy-done = f32[131072]{0:T(1024)S(1)} copy-done((f32[131072]{0:T(1024)S(1)}, f32[131072]{0:T(1024)}, u32[]{:S(2)}) %copy-start) | copy-done | bytes 524312
  1.7 60.4 %shard_map.59 = (f32[300,512]{1,0:T(8,128)S(1)}, f32[300,512]{1,0:T(8,128)S(1)}) custom-call(f32[300,512]{1,0:T(8,128)} %bitcast.6, f32[300,512]{1,0:T(8,128)} %bitcast.7, s32[2,512,2048]{2,1,0:T(8,128)} %counts_ref.1, f32[1024,128]{1,0:T(8,128)S(1)} %bitcast.5), custom_call_target="tpu_custom_call" | custom-call | tf_op jit(solution)/shard_map/pallas_call | solution.py:357
  62.1 1.1 %shard_map.60 = (f32[300,512]{1,0:T(8,128)}, f32[300,512]{1,0:T(8,128)}) custom-call(f32[300,512]{1,0:T(8,128)S(1)} %get-tuple-element.6.rows_ref, f32[300,512]{1,0:T(8,128)S(1)} %get-tuple-element.7.cols_ref), custom_call_target="tpu_custom_call" | custom-call | tf_op jit(solution)/shard_map/pallas_call | solution.py:401
Async XLA Ops:
  0.6 1.0 %copy-start = (f32[131072]{0:T(1024)S(1)}, f32[131072]{0:T(1024)}, u32[]{:S(2)}) copy-start(f32[131072]{0:T(1024)} %param.7) | copy-start | bytes 1572868
